TPU v7x, 32 devices: a whole 2x2x4 slice. The times are simulated.
32 devices in a mesh: segaz: 8 (over y, x, core), rad: 4 (over z).
Axes of the slice: x: 2, y: 2, z: 4, core: 2. Of those that a mesh axis runs over, the one named last changes fastest.
Arguments:
- state: float32 [5, 2048, 1024], P(None, 'segaz', 'rad'), may hold values from -6 to 6
- kappa: float32 [2048, 1024], P('segaz', 'rad'), may hold values from 0.1 to 1
- drop_src: float32 [5, 1048576], P(None, ('segaz', 'rad')), may hold values from -48 to 48
- drop_cell: int32 [1048576], P(('segaz', 'rad')), may hold values from 0 to 65535
- drop_count: int32 [32, 8], P(('segaz', 'rad')), may hold values from 1 to 5120, 32768 in all within a row
- part_map: int32 [8], replicated, may hold values from 0 to 7, as said below
- match_block: int32 [8], replicated, may hold values from 0 to 7, as said below
Outputs:
- new_state: float32 [5, 2048, 1024], P(None, 'segaz', 'rad')
Inputs may be any that keep to these rules, and one draw needn't show every extreme that they name: Each row of drop_count sums to 32768; a partition's droplet rows are grouped by destination in increasing segaz index: its first drop_count[p, 0] rows go to index 0, the next drop_count[p, 1] to index 1, and so on. Every row reaches the maximum. `part_map`: A permutation of the block ids. match_block[match_block[b]] = b and match_block[b] != b for every block b.
All inputs are finite; a program needn't handle non-finite values.
Results may differ from a plain program's by a relative error of at most 0.0003.
Values sent between devices are 32-bit elements; how exact they have to be, the bound alone decides.
No kernel may reach another device: no remote copies, remote signals or barrier semaphores. Data moves between devices by JAX's collectives and lax.ppermute only.
A program may use at most 128 MiB of HBM per device.

v0:
```python
import functools

import jax
import jax.numpy as jnp
import numpy as np
from jax import lax
from jax.experimental import pallas as pl
from jax.experimental.pallas import tpu as pltpu
from jax.sharding import PartitionSpec as P

FW = 4
JL = 4
LANES = 128
WINDOW = 32
ROUNDS = 3
UNROLL = 16
OWN_UNROLL = 5
STEP = 4
PIECES = 4
HALF = 64

time_step = 0.25
layer_weights = (1.0, 0.6, 0.35, 0.2)


def filter_weights(half_width):
    offsets = np.arange(-half_width, half_width + 1).astype(np.float32)
    bell_curve = np.exp(-offsets * offsets / np.float32(8.0))
    return bell_curve / np.sum(bell_curve)


def taps(targets, length):
    weights = filter_weights(FW)
    table = np.zeros((len(targets), length), np.float32)
    for i, cell in enumerate(targets):
        if cell is not None:
            for k in range(-FW, FW + 1):
                if 0 <= cell + k < length:
                    table[i, cell + k] = weights[k + FW]
    return table


def edge_targets(length):
    gap = [None] * (8 - FW)
    return list(range(-FW, 0)) + gap + list(range(length, length + FW)) + gap


def extended_targets(length):
    gap = [None] * (LANES - FW)
    return list(range(length)) + gap + list(range(-FW, 0)) + list(range(length, length + FW)) + gap


def pick_columns(radial):
    table = np.zeros((16, 2 * radial), np.float32)
    for k in range(FW):
        table[k, k] = 1.0
        table[8 + k, radial - FW + k] = 1.0
    table[FW, radial] = 1.0
    table[8 + FW, 2 * radial - 1] = 1.0
    return table


def halves(x):
    high = x.astype(jnp.bfloat16)
    return high, (x - high.astype(jnp.float32)).astype(jnp.bfloat16)


def product(x, y, dims):
    xh, xl = halves(x) if not isinstance(x, tuple) else x
    yh, yl = halves(y) if not isinstance(y, tuple) else y

    def dot(p, q):
        return lax.dot_general(p, q, (dims, ((), ())), preferred_element_type=jnp.float32)

    both = dot(jnp.concatenate([xh, xl], axis=0), yh)
    count = xh.shape[0]
    return both[:count] + (both[count:] + dot(xh, yl))


PLAIN = ((1,), (0,))
TURNED = ((1,), (1,))


def comparators(count):
    size = 1 << (count - 1).bit_length()
    pairs = []
    p = 1
    while p < size:
        k = p
        while k >= 1:
            for j in range(k % p, size - k, 2 * k):
                for i in range(min(k, size - j - k)):
                    if (i + j) // (2 * p) == (i + j + k) // (2 * p) and i + j + k < count:
                        pairs.append((i + j, i + j + k))
            k //= 2
        p *= 2
    return pairs


def sort_rows(tiles):
    pairs = comparators(len(tiles))
    for low, high in pairs:
        swap = tiles[high][-1] < tiles[low][-1]
        first = [jnp.where(swap, y, x) for x, y in zip(tiles[low], tiles[high])]
        second = [jnp.where(swap, x, y) for x, y in zip(tiles[low], tiles[high])]
        tiles[low], tiles[high] = first, second
    return tiles


class Slots:
    def __init__(self, components, cap_tiles, step):
        self.fields = components + 1
        self.cap_tiles, self.step = cap_tiles, step
        self.chunks = cap_tiles // step
        self.chunk_rows = self.fields * step
        self.face = -(-(8 + self.chunks * self.chunk_rows) // 8) * 8
        self.rows = self.face + 8 * components

    def place(self, j):
        return 8 + j * self.chunk_rows


def pack_kernel(
    slots, azim,
    count_hbm, src_hbm, cell_hbm, state_hbm, *refs,
):
    sends_hbm, count_ref, src_ref, cell_ref, face_ref, out_ref, held_ref, in_sems, out_sems = refs
    cap_tiles, step = slots.cap_tiles, slots.step
    components, row_count = src_ref.shape
    fields = components + 1
    tile_count = cell_ref.shape[0]
    radial = face_ref.shape[2]
    seg_count = sends_hbm.shape[0]
    piece = row_count // PIECES
    loads = [
        pltpu.make_async_copy(count_hbm, count_ref, in_sems.at[0]),
        pltpu.make_async_copy(state_hbm.at[:, 0:8, :], face_ref, in_sems.at[1]),
        pltpu.make_async_copy(cell_hbm, cell_ref, in_sems.at[2]),
    ] + [
        pltpu.make_async_copy(
            src_hbm.at[:, k * piece : (k + 1) * piece], src_ref.at[:, k * piece : (k + 1) * piece], in_sems.at[3 + k]
        )
        for k in range(PIECES)
    ]
    for load in loads:
        load.start()
    for load in loads:
        load.wait()
    lane = lax.broadcasted_iota(jnp.int32, (8, LANES), 1)
    sub = lax.broadcasted_iota(jnp.int32, (8, LANES), 0)
    none = float(azim * radial)

    def slot(g, begin):
        count = count_ref[0, g]
        first = begin // LANES
        shift = begin % LANES
        turn = (LANES - shift) % LANES

        def rolled(i):
            t = jnp.minimum(first + i, tile_count - 1)
            src = src_ref[:, pl.ds(pl.multiple_of(t * LANES, LANES), LANES)]
            cell = cell_ref[pl.ds(t, 1), :].astype(jnp.float32)
            both = jnp.concatenate([src, cell, jnp.zeros((8 - fields, LANES), jnp.float32)], axis=0)
            return pltpu.roll(both, turn, 1)

        row = g * slots.rows + slots.face
        for v in range(components):
            for half in range(2):
                out_ref[pl.ds(row + 8 * v + 4 * half, JL), :] = face_ref[
                    v, 0:JL, half * LANES : (half + 1) * LANES
                ]
        head = rolled(0)
        for i in range(cap_tiles):
            tail = rolled(i + 1)
            rows = jnp.where(lane < LANES - shift, head, tail)
            dead = (sub == components) & (lane >= count - i * LANES)
            rows = jnp.where(dead, none, rows)
            held_ref[g // 8, i, pl.ds(g % 8, 8, stride=8), :] = rows
            head = tail
        return begin + count

    lax.fori_loop(0, seg_count, slot, jnp.int32(0))

    def group(h):
        tiles = [
            [held_ref[h, i, 8 * f : 8 * f + 8, :] for f in range(fields)] for i in range(cap_tiles)
        ]
        tiles = sort_rows(tiles)
        for again in range(ROUNDS - 1):
            tiles = [[pltpu.roll(x, (37 * i) % LANES, 1) for x in tiles[i]] for i in range(cap_tiles)]
            tiles = sort_rows(tiles)
        bounds = jnp.zeros((8, LANES), jnp.float32)
        for i in range(cap_tiles):
            key = tiles[i][-1]
            least = jnp.min(key, axis=1, keepdims=True)
            most = jnp.max(jnp.where(key < none, key, -1.0), axis=1, keepdims=True)
            bounds = jnp.where(lane == i, jnp.floor(least * (1.0 / radial)), bounds)
            bounds = jnp.where(lane == HALF + i, jnp.floor(most * (1.0 / radial)), bounds)
        row = h * 8 * slots.rows
        out_ref[pl.ds(row, 8, stride=slots.rows), :] = bounds
        for i in range(cap_tiles):
            begin = row + slots.place(i // step) + fields * (i % step)
            for f in range(fields):
                out_ref[pl.ds(begin + f, 8, stride=slots.rows), :] = tiles[i][f]

    stores = []
    for h in range(seg_count // 8):
        group(h)
        for g in range(8 * h, 8 * h + 8):
            store = pltpu.make_async_copy(
                out_ref.at[g * slots.rows : (g + 1) * slots.rows, :], sends_hbm.at[g], out_sems.at[g]
            )
            store.start()
            stores.append(store)
    for store in stores:
        store.wait()


def base_kernel(state_ref, kappa_ref, out_ref, edge_ref):
    components, azim, radial = state_ref.shape
    lane = lax.broadcasted_iota(jnp.int32, (azim, radial), 1)
    sub = lax.broadcasted_iota(jnp.int32, (8, radial), 0)
    first = lane[:1] == 0
    last = lane[:1] == radial - 1
    pick = lax.broadcasted_iota(jnp.int32, (8, radial), 1)
    pick = ((sub == 2) & (pick == 0)) | ((sub == 3) & (pick == radial - 1))
    pick = jnp.where(pick, 1.0, 0.0).astype(jnp.bfloat16)
    none = jnp.zeros((1, radial), jnp.float32)

    def component(v, carry):
        q = state_ref[v]
        both = jnp.concatenate([q[1:], none], axis=0) + jnp.concatenate([none, q[:-1]], axis=0)
        column = both + 4.0 * q
        side = jnp.where(lane == radial - 1, 0.0, pltpu.roll(column, radial - 1, 1)) + jnp.where(
            lane == 0, 0.0, pltpu.roll(column, 1, 1)
        )
        total = side + (4.0 * both - 20.0 * q)
        out_ref[v] = q + time_step * (kappa_ref[...] * total / 6.0)

        def along(row):
            right = jnp.where(last, 0.0, pltpu.roll(row, radial - 1, 1))
            left = jnp.where(first, 0.0, pltpu.roll(row, 1, 1))
            return 4.0 * row + right + left

        top, bottom = q[:1], q[-1:]
        high, low = halves(column)
        turned = sum(
            lax.dot_general(pick, x, (TURNED, ((), ())), preferred_element_type=jnp.float32) for x in (high, low)
        )
        edge_ref[v] = jnp.where(
            sub == 0,
            along(top),
            jnp.where(sub == 1, along(bottom), jnp.where(sub == 4, top, jnp.where(sub == 5, bottom, turned))),
        )
        return carry

    lax.fori_loop(0, components, component, 0)


def by_least(slots, live, keys):
    columns = keys.T
    count, rows = keys.shape[0], slots.cap_tiles
    deep = -(-rows // 8) * 8
    length = -(-count * rows // LANES) * LANES
    slot = lax.broadcasted_iota(jnp.int32, keys.shape, 0)
    row = lax.broadcasted_iota(jnp.int32, keys.shape, 1)
    keys = (jnp.where(live, keys, 600.0) * (HALF * count)) + (slot * HALF + row).astype(jnp.float32)
    turned = keys.T
    places = []
    for s in range(count):
        fewer = jnp.zeros((deep, LANES), jnp.float32)
        for other in range(count):
            column = turned[:deep, other : other + 1]
            fewer += jnp.where(column < keys[s : s + 1, :], 1.0, 0.0)
        if deep > rows:
            extra = sum(
                jnp.where(turned[rows:deep, other : other + 1] < keys[s : s + 1, :], 1.0, 0.0)
                for other in range(count)
            )
            places.append(jnp.sum(fewer, axis=0, keepdims=True) - jnp.sum(extra, axis=0, keepdims=True))
        else:
            places.append(jnp.sum(fewer, axis=0, keepdims=True))
    places = jnp.concatenate(places, axis=0).T
    spot = lax.broadcasted_iota(jnp.int32, (deep, length), 1).astype(jnp.float32)
    name = lax.broadcasted_iota(jnp.int32, (deep, length), 0).astype(jnp.float32)
    tables = [jnp.zeros((deep, length), jnp.float32) for k in range(3)]
    for s in range(count):
        here = (places[:deep, s : s + 1] == spot) & (name < rows)
        values = (name + float(s * HALF), columns[:deep, s : s + 1], columns[HALF : HALF + deep, s : s + 1])
        tables = [table + jnp.where(here, value, 0.0) for table, value in zip(tables, values)]
    return [jnp.sum(table, axis=0, keepdims=True) for table in tables]


def by_window(step, count, least, most):
    length = least.shape[1]
    spot = lax.broadcasted_iota(jnp.int32, (1, length), 1)
    far = most
    for q in range(1, step):
        far = jnp.maximum(far, jnp.where(spot + q < count, pltpu.roll(most, length - q, 1), -1.0))
    start = jnp.floor(least * 0.125)
    windows = jnp.floor((far - 8.0 * start) * (1.0 / WINDOW)) + 1.0
    windows = jnp.where((spot % step == 0) & (spot < count), windows, 0.0)
    row = lax.broadcasted_iota(jnp.int32, (length, length), 0)
    earlier = jnp.where(row < lax.broadcasted_iota(jnp.int32, (length, length), 1), 1.0, 0.0).astype(jnp.bfloat16)
    sub = lax.broadcasted_iota(jnp.int32, (8, length), 0)

    def dot(x, y):
        return lax.dot_general(x.astype(jnp.bfloat16), y, (PLAIN, ((), ())), preferred_element_type=jnp.float32)

    before = dot(jnp.where(sub == 0, windows, 0.0), earlier)[:1]
    columns = jnp.where(sub == 0, before, jnp.where(sub == 1, before + windows, 0.0)).T
    items = work_length(length // step)
    item = lax.broadcasted_iota(jnp.int32, (length, items), 1).astype(jnp.float32)
    here = (columns[:, 0:1] <= item) & (item < columns[:, 1:2])
    here = jnp.where(here, 1.0, 0.0).astype(jnp.bfloat16)
    high = jnp.floor(before * (1.0 / 256))
    chunk = (spot // step).astype(jnp.float32)
    found = dot(
        jnp.where(
            sub == 0,
            chunk,
            jnp.where(sub == 1, start, jnp.where(sub == 2, high, jnp.where(sub == 3, before - 256.0 * high, 0.0))),
        ),
        here,
    )
    first = 8.0 * found[1:2] + WINDOW * (item[:1] - (256.0 * found[2:3] + found[3:4]))
    total = jnp.sum(windows).astype(jnp.int32)
    return found[0:1], first, total


def work_length(chunks):
    return -(-(chunks * (256 // WINDOW + 1) + UNROLL) // LANES) * LANES


def add_chunks(slots, own, own_only, got_ref, sum_ref, list_ref, task_ref, order_ref, work_ref, sems):
    seg_count = got_ref.shape[0]
    components, _, radial = sum_ref.shape
    azim = sum_ref.shape[1] - WINDOW
    fields, step = slots.fields, slots.step
    width = step * LANES
    count = -(-seg_count // 8) * 8
    bounds = [got_ref[s, 0:1, :] for s in range(seg_count)]
    if count > seg_count:
        bounds.append(jnp.full((count - seg_count, LANES), -1.0, jnp.float32))
    bounds = jnp.concatenate(bounds, axis=0)
    most = pltpu.roll(bounds, LANES - HALF, 1)
    live = (most >= 0) & (lax.broadcasted_iota(jnp.int32, (count, LANES), 1) < slots.cap_tiles)
    if not own_only:
        live = live & (lax.broadcasted_iota(jnp.int32, (count, LANES), 0) != own)
    total_rows = jnp.sum(jnp.where(live, 1.0, 0.0)).astype(jnp.int32)
    order, least, most = by_least(slots, live, bounds)
    list_ref[0:1, :] = order.astype(jnp.int32)
    chunk, first, total = by_window(step, total_rows, least, most)
    task_ref[0:1, :] = chunk.astype(jnp.int32)
    unroll = OWN_UNROLL if own_only else UNROLL
    task = lax.broadcasted_iota(jnp.int32, first.shape, 1)
    task_ref[1:2, :] = jnp.where(task < total, first.astype(jnp.int32), azim)
    copies = [
        pltpu.make_async_copy(task_ref, work_ref, sems.at[0]),
        pltpu.make_async_copy(list_ref, order_ref, sems.at[1]),
    ]
    for copy in copies:
        copy.start()
    cells = lax.broadcasted_iota(jnp.int32, (radial, width), 0).astype(jnp.float32).astype(jnp.bfloat16)
    near = lax.broadcasted_iota(jnp.int32, (WINDOW, width), 0).astype(jnp.float32).astype(jnp.bfloat16)
    lanes = lax.broadcasted_iota(jnp.int32, (1, width), 1)
    none = float(azim * radial)
    for copy in copies:
        copy.wait()

    def block(t):
        c = work_ref[0, t]
        start = pl.multiple_of(work_ref[1, t], 8)
        rows = []
        for q in range(step):
            name = order_ref[0, c * step + q]
            rows.append(got_ref[name // HALF, pl.ds(8 + fields * (name % HALF), fields), :])

        def field(k):
            return jnp.concatenate([x[k : k + 1] for x in rows], axis=1)

        ids = jnp.where(lanes < (total_rows - c * step) * LANES, field(components), none)
        a = jnp.floor(ids * (1.0 / radial))
        b = (ids - radial * a).astype(jnp.bfloat16)
        right = jnp.where(cells == b, jnp.bfloat16(1), jnp.bfloat16(0))
        in_a = near == (a - start.astype(jnp.float32)).astype(jnp.bfloat16)
        highs, lows = [], []
        for v in range(components):
            values = field(v)
            high = values.astype(jnp.bfloat16)
            low = (values - high.astype(jnp.float32)).astype(jnp.bfloat16)
            highs.append(jnp.where(in_a, high, jnp.bfloat16(0)))
            lows.append(jnp.where(in_a, low, jnp.bfloat16(0)))
        left = jnp.concatenate(highs + lows, axis=0)
        part = lax.dot_general(left, right, (TURNED, ((), ())), preferred_element_type=jnp.float32)
        part = part[: components * WINDOW] + part[components * WINDOW :]
        return start, part

    def several(t, carry):
        done = [block(t * unroll + u) for u in range(unroll)]
        for start, part in done:
            for v in range(components):
                sum_ref[v, pl.ds(start, WINDOW), :] += part[v * WINDOW : (v + 1) * WINDOW]
        return carry

    lax.fori_loop(0, (total + unroll - 1) // unroll, several, 0)


def own_kernel(slots, sends_hbm, sum_ref, held_ref, *work):
    own = lax.axis_index("segaz")
    load = pltpu.make_async_copy(sends_hbm.at[own], held_ref.at[0], work[-1])
    load.start()
    sum_ref[...] = jnp.zeros(sum_ref.shape, jnp.float32)
    load.wait()
    add_chunks(slots, own, True, held_ref, sum_ref, *work[:-1])


def rest_kernel(
    slots,
    map_ref, match_ref, got_ref, begun_ref, face_ref, edge_ref, near_ref, far_ref,
    sum_ref, joint_ref, before_ref, after_ref, side_ref,
    *work,
):
    seg_count = got_ref.shape[0]
    components, _, radial = sum_ref.shape
    azim = sum_ref.shape[1] - WINDOW
    sum_ref[...] = begun_ref[...]
    own = lax.axis_index("segaz")
    add_chunks(slots, own, False, got_ref, sum_ref, *work)

    partner = jnp.int32(0)
    target = match_ref[map_ref[own]]
    for h in range(seg_count):
        partner = jnp.where(map_ref[h] == target, h, partner)
    layer = lax.broadcasted_iota(jnp.int32, (JL, radial), 0)
    strength = jnp.zeros((JL, radial), jnp.float32)
    for l in range(JL):
        strength = jnp.where(layer == l, layer_weights[l], strength)
    for v in range(components):
        tile = got_ref[partner, slots.face + 8 * v : slots.face + 8 * v + 8, :]
        face = jnp.concatenate([tile[:JL], tile[JL:]], axis=1)
        joint_ref[v, 0:JL, :] = strength * (face - face_ref[v, 0:JL, :])
        joint_ref[v, JL:8, :] = jnp.zeros((8 - JL, radial), jnp.float32)

    near = halves(near_ref[...])
    far = halves(far_ref[...])
    inner = tuple(x[:, :radial] for x in far)
    ends = tuple(jnp.concatenate([x[:, :16], x[:, azim - 16 :]], axis=1) for x in near)
    rows, columns = [], []
    for v in range(components):
        cells_v = halves(sum_ref[v, 0:azim, :])
        edges = tuple(jnp.concatenate([x[:16], x[azim - 16 :]], axis=0) for x in cells_v)
        rows.append(product(ends, edges, PLAIN))
        columns.append(product(near, cells_v, TURNED))
    rows = product(jnp.concatenate(rows, axis=0), inner, PLAIN)
    columns = product(jnp.concatenate(columns, axis=0), far, PLAIN)
    sub = lax.broadcasted_iota(jnp.int32, (8, LANES), 0)
    lane = lax.broadcasted_iota(jnp.int32, (8, LANES), 1)
    half = LANES
    for v in range(components):
        row = rows[16 * v : 16 * v + 16]
        column = columns[16 * v : 16 * v + 16]
        edge = edge_ref[v]
        wide = lax.broadcasted_iota(jnp.int32, (8, radial), 0)
        after_ref[v, :, :radial] = jnp.where(wide == FW, edge[1:2], row[8:16])
        before_ref[v, :, :radial] = jnp.where(
            wide == FW - 1, edge[0:1], jnp.concatenate([row[FW:8], row[0:FW]], axis=0)
        )
        bottom, top = edge[5:6], edge[4:5]
        left_corner = jnp.where(lane[:1] == 0, bottom[:, :half], 0.0)
        right_corner = jnp.where(lane[:1] == 0, pltpu.roll(bottom[:, radial - half :], 1, 1), 0.0)
        after_ref[v, :, radial : radial + half] = jnp.where(
            sub == FW, left_corner, column[0:8, radial + half : radial + 2 * half]
        )
        after_ref[v, :, radial + half : radial + 2 * half] = jnp.where(
            sub == FW, right_corner, column[8:16, radial + half : radial + 2 * half]
        )
        left_corner = jnp.where(lane[:1] == half - 1, pltpu.roll(top[:, :half], half - 1, 1), 0.0)
        right_corner = jnp.where(lane[:1] == half - 1, top[:, radial - half :], 0.0)
        before_ref[v, :, radial : radial + half] = jnp.where(
            sub == FW, left_corner, column[0:8, radial : radial + half]
        )
        before_ref[v, :, radial + half : radial + 2 * half] = jnp.where(
            sub == FW, right_corner, column[8:16, radial : radial + half]
        )
        side_ref[v, 0:8, :] = jnp.where(wide == FW, edge[2:3], column[0:8, :radial])
        side_ref[v, 8:16, :] = jnp.where(wide == FW, edge[3:4], column[8:16, :radial])


def inner_kernel(sum_ref, base_ref, joint_ref, band_ref, out_ref):
    components, azim, radial = base_ref.shape
    band = halves(band_ref[...])

    def component(v, carry):
        across = product(sum_ref[v, 0:azim, :], band, PLAIN)
        both = product(band, across, PLAIN)
        out_ref[v] = base_ref[v] + time_step * both
        out_ref[v, 0:8, :] += time_step * joint_ref[v]
        return carry

    lax.fori_loop(0, components, component, 0)


def corner_kernel(side_ref, prior_ref, next_ref, left_ref, right_ref):
    radial = left_ref.shape[2]
    for out_ref, begin, corner in ((left_ref, 0, radial), (right_ref, 8, radial + LANES)):
        out_ref[:, :, :LANES] = (
            side_ref[:, begin : begin + 8, :LANES] + prior_ref[:, :, corner : corner + LANES]
        )
        out_ref[:, :, LANES:] = (
            side_ref[:, begin : begin + 8, LANES:] + next_ref[:, :, corner : corner + LANES]
        )


def final_kernel(inner_ref, kappa_ref, prior_ref, next_ref, left_ref, right_ref, pick_ref, out_ref):
    v = pl.program_id(0)
    azim, radial = kappa_ref.shape
    pick = pick_ref[...].astype(jnp.bfloat16)
    sub = lax.broadcasted_iota(jnp.int32, (8, radial), 0)
    parts = halves(jnp.concatenate([left_ref[v], right_ref[v]], axis=0))
    sides = sum(
        lax.dot_general(x, pick, (((0,), (0,)), ((), ())), preferred_element_type=jnp.float32) for x in parts
    )
    kappa = kappa_ref[...]
    out_ref[0] = inner_ref[v] + time_step * (sides[:, :radial] + kappa * sides[:, radial:] / 6.0)
    prior = prior_ref[v, :, :radial]
    add = jnp.where(sub < FW, prior, 0.0) + jnp.where(sub == 0, kappa[0:8] * prior[FW : FW + 1] / 6.0, 0.0)
    out_ref[0, 0:8, :] += time_step * add
    nxt = next_ref[v, :, :radial]
    add = jnp.where(sub >= 8 - FW, nxt, 0.0) + jnp.where(
        sub == 7, kappa[azim - 8 : azim] * nxt[FW - 1 : FW] / 6.0, 0.0
    )
    out_ref[0, azim - 8 : azim, :] += time_step * add


def call(kernel, outs, ins, scratch=(), cost=None, to="vmem", room=48):
    spaces = {"smem": pltpu.SMEM, "vmem": pltpu.VMEM, "hbm": pltpu.HBM, "any": pl.ANY}

    def spec(where):
        if isinstance(where, str):
            return pl.BlockSpec(memory_space=spaces[where])
        return pl.BlockSpec(where, lambda i: (0,) * len(where))

    return pl.pallas_call(
        kernel,
        grid=(1,),
        out_shape=[jax.ShapeDtypeStruct(shape, jnp.float32) for shape in outs],
        in_specs=[spec(where) for where in ins],
        out_specs=[spec(to)] * len(outs),
        scratch_shapes=list(scratch),
        cost_estimate=None
        if cost is None
        else pl.CostEstimate(flops=cost, bytes_accessed=cost // 1000, transcendentals=0),
        compiler_params=pltpu.CompilerParams(vmem_limit_bytes=room << 20),
    )


def shifted(strip, axis, way):
    count = lax.axis_size(axis)
    pairs = [(i, i + 1) if way > 0 else (i + 1, i) for i in range(count - 1)]
    return lax.ppermute(strip, axis, pairs)


def local(state, kappa, drop_src, drop_cell, drop_count, part_map, match_block):
    components, azim, radial = state.shape
    row_count = drop_src.shape[1]
    seg_count = lax.axis_size("segaz")
    capacity = 5 * row_count // (4 * seg_count)
    cap_tiles = capacity // LANES
    slots = Slots(components, cap_tiles, STEP if cap_tiles % STEP == 0 else 2)
    face = (components, 8, radial)
    whole = state.shape
    sums = (components, azim + WINDOW, radial)
    strip = (components, 8, 2 * radial)
    sides = (components, 8, radial)
    (sends,) = call(
        functools.partial(pack_kernel, slots, azim),
        [(seg_count, slots.rows, LANES)],
        ["hbm"] * 4,
        [
            pltpu.SMEM(drop_count.shape[:1] + (seg_count,), jnp.int32),
            pltpu.VMEM(drop_src.shape, jnp.float32),
            pltpu.VMEM((row_count // LANES, LANES), jnp.int32),
            pltpu.VMEM(face, jnp.float32),
            pltpu.VMEM((seg_count * slots.rows, LANES), jnp.float32),
            pltpu.VMEM((seg_count // 8, cap_tiles, 64, LANES), jnp.float32),
            pltpu.SemaphoreType.DMA((3 + PIECES,)),
            pltpu.SemaphoreType.DMA((seg_count,)),
        ],
        to="hbm",
        room=62,
    )(drop_count, drop_src, drop_cell.reshape(-1, LANES), state)
    got = lax.all_to_all(sends, "segaz", split_axis=0, concat_axis=0, tiled=True)

    def work(count):
        length = -(-(-(-count // 8) * 8) * cap_tiles // LANES) * LANES
        return [
            pltpu.VMEM((8, length), jnp.int32),
            pltpu.VMEM((8, work_length(length // slots.step)), jnp.int32),
            pltpu.SMEM((8, length), jnp.int32),
            pltpu.SMEM((8, work_length(length // slots.step)), jnp.int32),
            pltpu.SemaphoreType.DMA((2,)),
        ]

    (begun,) = call(
        functools.partial(own_kernel, slots),
        [sums],
        ["hbm"],
        [pltpu.VMEM((1, slots.rows, LANES), jnp.float32)] + work(1) + [pltpu.SemaphoreType.DMA(())],
        cost=1 << 23,
    )(sends)
    still, edge = call(base_kernel, [whole, face], ["vmem", "vmem"], cost=1 << 22)(state, kappa)
    near = jnp.asarray(taps(edge_targets(azim), azim))
    far = jnp.asarray(taps(extended_targets(azim), azim).T)
    band = jnp.asarray(taps(list(range(azim)), azim))
    source, joint, before, after, side = call(
        functools.partial(rest_kernel, slots),
        [sums, face, strip, strip, (components, 16, radial)],
        ["smem", "smem", "vmem", "vmem", face, "vmem", "vmem", "vmem"],
        work(seg_count),
    )(part_map, match_block, got, begun, state, edge, near, far)
    prior = shifted(after, "segaz", 1)
    nxt = shifted(before, "segaz", -1)
    (inner,) = call(inner_kernel, [whole], ["vmem"] * 4, cost=1 << 22)(source, still, joint, band)
    to_left, to_right = call(corner_kernel, [sides, sides], ["vmem"] * 3)(side, prior, nxt)
    left = shifted(to_right, "rad", 1)
    right = shifted(to_left, "rad", -1)
    pick = jnp.asarray(pick_columns(radial))
    return pl.pallas_call(
        final_kernel,
        grid=(components,),
        out_shape=jax.ShapeDtypeStruct(whole, jnp.float32),
        in_specs=[pl.BlockSpec(memory_space=pltpu.VMEM)] * 7,
        out_specs=pl.BlockSpec((1, azim, radial), lambda v: (v, 0, 0)),
        compiler_params=pltpu.CompilerParams(vmem_limit_bytes=48 << 20),
    )(inner, kappa, prior, nxt, left, right, pick)


def solution(mesh):
    return jax.shard_map(
        local,
        mesh=mesh,
        in_specs=(
            P(None, "segaz", "rad"),
            P("segaz", "rad"),
            P(None, ("segaz", "rad")),
            P(("segaz", "rad")),
            P(("segaz", "rad"), None),
            P(),
            P(),
        ),
        out_specs=P(None, "segaz", "rad"),
        check_vma=False,
    )
```

profile of v0, /device:TPU:19, one launch (start us, length us, event | category | flops | bytes accessed | tf_op | source)
XLA Modules:
  0.0 67.8 jit_solution(8526005696015641940)
XLA Ops:
  0.0 6.9 %shard_map.109.sends_hbm = f32[8,288,128]{2,1,0:T(8,128)} custom-call(s32[1,8]{1,0:T(1,128)} %count_hbm.1, f32[5,32768]{1,0:T(8,128)} %src_hbm.1, s32[256,128]{1,0:T(8,128)} %bitcast.1, f32[5,256,256]{2,1,0:T(8,128)} %face_ref.1), custom_call_target="tpu_custom_call" | custom-call | tf_op jit(solution)/shard_map/pallas_call | solution.py:576
  6.9 0.0 copy-start
  6.9 0.0 copy-start.5
  6.9 5.1 %all-to-all-start = ((f32[8,288,128]{2,1,0:T(8,128)}), f32[8,288,128]{2,1,0:T(8,128)}, u32[]{:S(2)}, u32[]{:S(2)}) async-start(f32[8,288,128]{2,1,0:T(8,128)} %shard_map.109.sends_hbm), calls=%async_computation | async-start | bytes 2359296 | tf_op jit(solution)/shard_map/all_to_all | solution.py:593
  12.1 0.0 copy-done
  12.1 0.0 copy-done.5
  12.1 0.0 copy-start.1
  12.1 1.3 %shard_map.111 = (f32[5,256,256]{2,1,0:T(8,128)S(1)}, f32[5,8,256]{2,1,0:T(8,128)S(1)}) custom-call(f32[5,256,256]{2,1,0:T(8,128)S(1)} %copy-done, f32[256,256]{1,0:T(8,128)S(1)} %copy-done.5), custom_call_target="tpu_custom_call" | custom-call | flops 4194304 | bytes 4194 | tf_op jit(solution)/shard_map/pallas_call | solution.py:612
  13.4 0.0 copy-start.3
  13.4 1.0 %copy-done.3 = f32[5,256,256]{2,1,0:T(8,128)} copy-done((f32[5,256,256]{2,1,0:T(8,128)}, f32[5,256,256]{2,1,0:T(8,128)S(1)}, u32[]{:S(2)}) %copy-start.3) | copy-done | bytes 1310744
  14.5 0.0 copy-done.1
  14.5 0.0 copy-start.6
  14.5 0.0 copy-start.9
  14.5 0.0 copy-start.10
  14.5 0.0 copy-start.11
  14.5 5.0 %shard_map.110.begun_ref = f32[5,288,256]{2,1,0:T(8,128)S(1)} custom-call(f32[8,288,128]{2,1,0:T(8,128)S(1)} %copy-done.1), custom_call_target="tpu_custom_call" | custom-call | flops 8388608 | bytes 8388 | tf_op jit(solution)/shard_map/pallas_call | solution.py:605
  19.5 0.0 copy-start.2
  19.5 1.1 %copy-done.2 = f32[5,288,256]{2,1,0:T(8,128)} copy-done((f32[5,288,256]{2,1,0:T(8,128)}, f32[5,288,256]{2,1,0:T(8,128)S(1)}, u32[]{:S(2)}) %copy-start.2) | copy-done | bytes 1474584
  20.7 6.8 %all-to-all-done.got_ref = f32[8,288,128]{2,1,0:T(8,128)} async-done(((f32[8,288,128]{2,1,0:T(8,128)}), f32[8,288,128]{2,1,0:T(8,128)}, u32[]{:S(2)}, u32[]{:S(2)}) %all-to-all-start) | async-done | bytes 1179680 | tf_op jit(solution)/shard_map/all_to_all | solution.py:593
  27.4 0.0 copy-done.6
  27.4 0.0 copy-done.9
  27.4 0.0 copy-done.10
  27.4 0.0 copy-done.11
  27.4 0.0 copy-start.4
  27.4 0.0 copy-start.7
  27.5 18.3 %shard_map.112 = (f32[5,288,256]{2,1,0:T(8,128)S(1)}, f32[5,8,256]{2,1,0:T(8,128)S(1)}, f32[5,8,512]{2,1,0:T(8,128)S(1)}, f32[5,8,512]{2,1,0:T(8,128)S(1)}, f32[5,16,256]{2,1,0:T(8,128)S(1)}) custom-call(s32[8]{0:T(128)S(1)} %copy-done.10, s32[8]{0:T(128)S(1)} %copy-done.11, f32[8,288,128]{2,1,0:T(8,128)} %all-to-all-done.got_ref, f32[5,288,256]{2,1,0:T(8,128)} %copy-done.2, ...), custom_call_target="tpu_custom_call" | custom-call | tf_op jit(solution)/shard_map/pallas_call | solution.py:616
  45.8 3.4 %collective-permute-start = (f32[5,8,512]{2,1,0:T(8,128)S(1)}, f32[5,8,512]{2,1,0:T(8,128)S(1)}, u32[]{:S(2)}, u32[]{:S(2)}) collective-permute-start(f32[5,8,512]{2,1,0:T(8,128)S(1)} %get-tuple-element.18), channel_id=1, source_target_pairs={{0,4},{4,8},{8,12},{12,16},{16,20},{20,24},{24,28},{1,5},{5,9},{9,... | collective-permute-start | bytes 245768 | tf_op jit(solution)/shard_map/ppermute | solution.py:561
  49.2 1.9 %collective-permute-start.1 = (f32[5,8,512]{2,1,0:T(8,128)S(1)}, f32[5,8,512]{2,1,0:T(8,128)S(1)}, u32[]{:S(2)}, u32[]{:S(2)}) collective-permute-start(f32[5,8,512]{2,1,0:T(8,128)S(1)} %get-tuple-element.19), channel_id=1, source_target_pairs={{4,0},{8,4},{12,8},{16,12},{20,16},{24,20},{28,24},{5,1},{9,5},{13... | collective-permute-start | bytes 245768 | tf_op jit(solution)/shard_map/ppermute | solution.py:561
  51.1 0.0 collective-permute-done.prior_ref
  51.2 4.7 %collective-permute-done.1.next_ref = f32[5,8,512]{2,1,0:T(8,128)S(1)} collective-permute-done((f32[5,8,512]{2,1,0:T(8,128)S(1)}, f32[5,8,512]{2,1,0:T(8,128)S(1)}, u32[]{:S(2)}, u32[]{:S(2)}) %collective-permute-start.1) | collective-permute-done | bytes 81952 | tf_op jit(solution)/shard_map/ppermute | solution.py:561
  55.9 3.2 %collective-permute-start.2 = (f32[5,8,256]{2,1,0:T(8,128)S(1)}, f32[5,8,256]{2,1,0:T(8,128)S(1)}, u32[]{:S(2)}, u32[]{:S(2)}) collective-permute-start(f32[5,8,256]{2,1,0:T(8,128)S(1)} %get-tuple-element.21), channel_id=1, source_target_pairs={{0,1},{1,2},{2,3},{4,5},{5,6},{6,7},{8,9},{9,10},{10,11},{12,13},{... | collective-permute-start | bytes 122888 | tf_op jit(solution)/shard_map/ppermute | solution.py:561
  59.1 2.1 %collective-permute-start.3 = (f32[5,8,256]{2,1,0:T(8,128)S(1)}, f32[5,8,256]{2,1,0:T(8,128)S(1)}, u32[]{:S(2)}, u32[]{:S(2)}) collective-permute-start(f32[5,8,256]{2,1,0:T(8,128)S(1)} %get-tuple-element.22), channel_id=1, source_target_pairs={{1,0},{2,1},{3,2},{5,4},{6,5},{7,6},{9,8},{10,9},{11,10},{13,12},{... | collective-permute-start | bytes 122888 | tf_op jit(solution)/shard_map/ppermute | solution.py:561
  61.2 0.0 copy-done.4
  61.2 0.0 copy-done.7
  61.2 0.0 copy-start.8
  61.2 3.4 %shard_map.113.inner_ref = f32[5,256,256]{2,1,0:T(8,128)S(1)} custom-call(f32[5,288,256]{2,1,0:T(8,128)S(1)} %get-tuple-element.15.sum_ref, f32[5,256,256]{2,1,0:T(8,128)S(1)} %copy-done.4, f32[5,8,256]{2,1,0:T(8,128)S(1)} %get-tuple-element.17.joint_ref, f32[256,256]{1,0:T(8,128)S(1)} %copy-done.7), custom_call_target="tpu_custom_call" | custom-call | flops 4194304 | bytes 4194 | tf_op jit(solution)/shard_map/pallas_call | solution.py:624
  64.7 0.0 collective-permute-done.2.left_ref
  64.7 0.0 collective-permute-done.3.right_ref
  64.7 0.0 copy-done.8
  64.7 3.1 %shard_map.115 = f32[5,256,256]{2,1,0:T(8,128)} custom-call(f32[5,256,256]{2,1,0:T(8,128)S(1)} %shard_map.113.inner_ref, f32[256,256]{1,0:T(8,128)S(1)} %copy-done.5, f32[5,8,512]{2,1,0:T(8,128)S(1)} %collective-permute-done.prior_ref, f32[5,8,512]{2,1,0:T(8,128)S(1)} %collective-permute-done.1.next_ref, f32[5,8,256]{2,1,0:T(8,128)S(1)} %collective-permute-done.2.left_ref, ...), custom_call_target="tpu_custom_call" | custom-call | tf_op jit(solution)/shard_map/pallas_call | solution.py:629
  (1 shorter events, 0.0 us)
Async XLA Ops:
  6.9 5.1 %copy-start = (f32[5,256,256]{2,1,0:T(8,128)S(1)}, f32[5,256,256]{2,1,0:T(8,128)}, u32[]{:S(2)}) copy-start(f32[5,256,256]{2,1,0:T(8,128)} %face_ref.1) | copy-start | bytes 3932164
  6.9 5.1 %copy-start.5 = (f32[256,256]{1,0:T(8,128)S(1)}, f32[256,256]{1,0:T(8,128)}, u32[]{:S(2)}) copy-start(f32[256,256]{1,0:T(8,128)} %kappa_ref.3) | copy-start | bytes 786436
  6.9 20.5 %all-to-all-start = ((f32[8,288,128]{2,1,0:T(8,128)}), f32[8,288,128]{2,1,0:T(8,128)}, u32[]{:S(2)}, u32[]{:S(2)}) async-start(f32[8,288,128]{2,1,0:T(8,128)} %shard_map.109.sends_hbm), calls=%async_computation | async-start | bytes 2359296 | tf_op jit(solution)/shard_map/all_to_all | solution.py:593
  12.1 2.4 %copy-start.1 = (f32[8,288,128]{2,1,0:T(8,128)S(1)}, f32[8,288,128]{2,1,0:T(8,128)}, u32[]{:S(2)}) copy-start(f32[8,288,128]{2,1,0:T(8,128)} %shard_map.109.sends_hbm) | copy-start | bytes 3538948
  13.4 1.1 %copy-start.3 = (f32[5,256,256]{2,1,0:T(8,128)}, f32[5,256,256]{2,1,0:T(8,128)S(1)}, u32[]{:S(2)}) copy-start(f32[5,256,256]{2,1,0:T(8,128)S(1)} %get-tuple-element.16.base_ref) | copy-start | bytes 3932164
  14.5 12.9 %copy-start.6 = (f32[256,512]{1,0:T(8,128)S(1)}, f32[256,512]{1,0:T(8,128)}, u32[]{:S(2)}) copy-start(f32[256,512]{1,0:T(8,128)} %constant.9.clone.far_ref) | copy-start | bytes 1572868
  14.5 12.9 %copy-start.9 = (f32[16,256]{1,0:T(8,128)S(1)}, f32[16,256]{1,0:T(8,128)}, u32[]{:S(2)}) copy-start(f32[16,256]{1,0:T(8,128)} %constant.8.clone.near_ref) | copy-start | bytes 49156
  14.5 12.9 %copy-start.10 = (s32[8]{0:T(128)S(1)}, s32[8]{0:T(128)}, u32[]{:S(2)}) copy-start(s32[8]{0:T(128)} %map_ref.1) | copy-start | bytes 100
  14.5 12.9 %copy-start.11 = (s32[8]{0:T(128)S(1)}, s32[8]{0:T(128)}, u32[]{:S(2)}) copy-start(s32[8]{0:T(128)} %match_ref.1) | copy-start | bytes 100
  19.5 1.1 %copy-start.2 = (f32[5,288,256]{2,1,0:T(8,128)}, f32[5,288,256]{2,1,0:T(8,128)S(1)}, u32[]{:S(2)}) copy-start(f32[5,288,256]{2,1,0:T(8,128)S(1)} %shard_map.110.begun_ref) | copy-start | bytes 4423684
  27.4 33.8 %copy-start.4 = (f32[5,256,256]{2,1,0:T(8,128)S(1)}, f32[5,256,256]{2,1,0:T(8,128)}, u32[]{:S(2)}) copy-start(f32[5,256,256]{2,1,0:T(8,128)} %copy-done.3) | copy-start | bytes 3932164
  27.4 33.8 %copy-start.7 = (f32[256,256]{1,0:T(8,128)S(1)}, f32[256,256]{1,0:T(8,128)}, u32[]{:S(2)}) copy-start(f32[256,256]{1,0:T(8,128)} %constant.10.clone.band_ref) | copy-start | bytes 786436
  45.8 5.4 %collective-permute-start = (f32[5,8,512]{2,1,0:T(8,128)S(1)}, f32[5,8,512]{2,1,0:T(8,128)S(1)}, u32[]{:S(2)}, u32[]{:S(2)}) collective-permute-start(f32[5,8,512]{2,1,0:T(8,128)S(1)} %get-tuple-element.18), channel_id=1, source_target_pairs={{0,4},{4,8},{8,12},{12,16},{16,20},{20,24},{24,28},{1,5},{5,9},{9,... | collective-permute-start | bytes 245768 | tf_op jit(solution)/shard_map/ppermute | solution.py:561
  49.2 6.7 %collective-permute-start.1 = (f32[5,8,512]{2,1,0:T(8,128)S(1)}, f32[5,8,512]{2,1,0:T(8,128)S(1)}, u32[]{:S(2)}, u32[]{:S(2)}) collective-permute-start(f32[5,8,512]{2,1,0:T(8,128)S(1)} %get-tuple-element.19), channel_id=1, source_target_pairs={{4,0},{8,4},{12,8},{16,12},{20,16},{24,20},{28,24},{5,1},{9,5},{13... | collective-permute-start | bytes 245768 | tf_op jit(solution)/shard_map/ppermute | solution.py:561
  55.9 8.8 %collective-permute-start.2 = (f32[5,8,256]{2,1,0:T(8,128)S(1)}, f32[5,8,256]{2,1,0:T(8,128)S(1)}, u32[]{:S(2)}, u32[]{:S(2)}) collective-permute-start(f32[5,8,256]{2,1,0:T(8,128)S(1)} %get-tuple-element.21), channel_id=1, source_target_pairs={{0,1},{1,2},{2,3},{4,5},{5,6},{6,7},{8,9},{9,10},{10,11},{12,13},{... | collective-permute-start | bytes 122888 | tf_op jit(solution)/shard_map/ppermute | solution.py:561
  59.1 5.6 %collective-permute-start.3 = (f32[5,8,256]{2,1,0:T(8,128)S(1)}, f32[5,8,256]{2,1,0:T(8,128)S(1)}, u32[]{:S(2)}, u32[]{:S(2)}) collective-permute-start(f32[5,8,256]{2,1,0:T(8,128)S(1)} %get-tuple-element.22), channel_id=1, source_target_pairs={{1,0},{2,1},{3,2},{5,4},{6,5},{7,6},{9,8},{10,9},{11,10},{13,12},{... | collective-permute-start | bytes 122888 | tf_op jit(solution)/shard_map/ppermute | solution.py:561
  61.2 3.5 %copy-start.8 = (f32[16,512]{1,0:T(8,128)S(1)}, f32[16,512]{1,0:T(8,128)}, u32[]{:S(2)}) copy-start(f32[16,512]{1,0:T(8,128)} %constant.11.clone.pick_ref) | copy-start | bytes 98308
where the time goes:
time: 68.5 us; the launch traced here: 67.8 us
  Pallas kernels  38.1 us (56%)
  starting transfers between devices  15.8 us (23%)
  waiting for transfers between devices  11.5 us (17%)
  local copies, waits for them, and re-layouts  2.24 us (3%)
    pallas_call x1, Pallas kernels, local(): call(functools.partial(rest_kernel, slots), [sums, face, strip, strip, (c...  18.3 us
    ppermute x4, starting transfers between devices, shifted(): return lax.ppermute(strip, axis, pairs)  10.6 us
    pallas_call x1, Pallas kernels, local(): call(functools.partial(pack_kernel, slots, azim), [(seg_count, slots.rows...  6.91 us
    all_to_all x1, waiting for transfers between devices, local(): lax.all_to_all(sends, 'segaz', split_axis=0, concat_axis=0, tiled=True)  6.76 us
    all_to_all x1, starting transfers between devices, local(): lax.all_to_all(sends, 'segaz', split_axis=0, concat_axis=0, tiled=True)  5.12 us
    pallas_call x1, Pallas kernels, local(): call(functools.partial(own_kernel, slots), [sums], ['hbm'], [pltpu.VMEM((...  5.01 us
    ppermute x4, waiting for transfers between devices, shifted(): return lax.ppermute(strip, axis, pairs)  4.73 us
    pallas_call x1, Pallas kernels, local(): call(inner_kernel, [whole], ['vmem'] * 4, cost=1 << 22)  3.43 us
  transfers between devices with their start and end apart: 5, of which 2 were waited for; matrix products, arithmetic and copies ran while one was open for 0% of the time, Pallas kernels for 14%

commit v1 on v0

--- a/solution.py
+++ b/solution.py
@@ -11,8 +11,8 @@
 FW = 4
 JL = 4
 LANES = 128
-WINDOW = 32
-ROUNDS = 3
+WINDOW = 48
+ROUNDS = 6
 UNROLL = 16
 OWN_UNROLL = 5
 STEP = 4
@@ -97,8 +97,13 @@
     return pairs
 
 
-def sort_rows(tiles):
-    pairs = comparators(len(tiles))
+def touch_up(count):
+    return [
+        (i, i + d) for d in (2, 1) for odd in (0, 1) for i in range(count - d) if i // d % 2 == odd
+    ]
+
+
+def sort_rows(tiles, pairs):
     for low, high in pairs:
         swap = tiles[high][-1] < tiles[low][-1]
         first = [jnp.where(swap, y, x) for x, y in zip(tiles[low], tiles[high])]
@@ -185,10 +190,10 @@
         tiles = [
             [held_ref[h, i, 8 * f : 8 * f + 8, :] for f in range(fields)] for i in range(cap_tiles)
         ]
-        tiles = sort_rows(tiles)
-        for again in range(ROUNDS - 1):
+        tiles = sort_rows(tiles, comparators(cap_tiles))
+        for again in range(ROUNDS):
             tiles = [[pltpu.roll(x, (37 * i) % LANES, 1) for x in tiles[i]] for i in range(cap_tiles)]
-            tiles = sort_rows(tiles)
+            tiles = sort_rows(tiles, touch_up(cap_tiles))
         bounds = jnp.zeros((8, LANES), jnp.float32)
         for i in range(cap_tiles):
             key = tiles[i][-1]
@@ -235,7 +240,7 @@
             lane == 0, 0.0, pltpu.roll(column, 1, 1)
         )
         total = side + (4.0 * both - 20.0 * q)
-        out_ref[v] = q + time_step * (kappa_ref[...] * total / 6.0)
+        out_ref[v] = q + (time_step / 6.0) * (kappa_ref[...] * total)
 
         def along(row):
             right = jnp.where(last, 0.0, pltpu.roll(row, radial - 1, 1))
@@ -512,25 +517,34 @@
         )
 
 
-def final_kernel(inner_ref, kappa_ref, prior_ref, next_ref, left_ref, right_ref, pick_ref, out_ref):
-    v = pl.program_id(0)
-    azim, radial = kappa_ref.shape
+def final_kernel(inner_ref, kappa_ref, prior_ref, next_ref, left_ref, right_ref, pick_ref, out_hbm, out_ref, sems):
+    components, azim, radial = out_ref.shape
     pick = pick_ref[...].astype(jnp.bfloat16)
     sub = lax.broadcasted_iota(jnp.int32, (8, radial), 0)
-    parts = halves(jnp.concatenate([left_ref[v], right_ref[v]], axis=0))
-    sides = sum(
-        lax.dot_general(x, pick, (((0,), (0,)), ((), ())), preferred_element_type=jnp.float32) for x in parts
-    )
-    kappa = kappa_ref[...]
-    out_ref[0] = inner_ref[v] + time_step * (sides[:, :radial] + kappa * sides[:, radial:] / 6.0)
-    prior = prior_ref[v, :, :radial]
-    add = jnp.where(sub < FW, prior, 0.0) + jnp.where(sub == 0, kappa[0:8] * prior[FW : FW + 1] / 6.0, 0.0)
-    out_ref[0, 0:8, :] += time_step * add
-    nxt = next_ref[v, :, :radial]
-    add = jnp.where(sub >= 8 - FW, nxt, 0.0) + jnp.where(
-        sub == 7, kappa[azim - 8 : azim] * nxt[FW - 1 : FW] / 6.0, 0.0
-    )
-    out_ref[0, azim - 8 : azim, :] += time_step * add
+    stores = []
+    for v in range(components):
+        parts = halves(jnp.concatenate([left_ref[v], right_ref[v]], axis=0))
+        sides = sum(
+            lax.dot_general(x, pick, (((0,), (0,)), ((), ())), preferred_element_type=jnp.float32) for x in parts
+        )
+        kappa = kappa_ref[...]
+        total = inner_ref[v] + time_step * sides[:, :radial] + (time_step / 6.0) * (kappa * sides[:, radial:])
+        prior = prior_ref[v, :, :radial]
+        add = jnp.where(sub < FW, prior, 0.0) + jnp.where(
+            sub == 0, kappa[0:8] * (prior[FW : FW + 1] * (1.0 / 6.0)), 0.0
+        )
+        out_ref[v, 0:8, :] = total[0:8] + time_step * add
+        out_ref[v, 8 : azim - 8, :] = total[8 : azim - 8]
+        nxt = next_ref[v, :, :radial]
+        add = jnp.where(sub >= 8 - FW, nxt, 0.0) + jnp.where(
+            sub == 7, kappa[azim - 8 : azim] * (nxt[FW - 1 : FW] * (1.0 / 6.0)), 0.0
+        )
+        out_ref[v, azim - 8 : azim, :] = total[azim - 8 : azim] + time_step * add
+        store = pltpu.make_async_copy(out_ref.at[v], out_hbm.at[v], sems.at[v])
+        store.start()
+        stores.append(store)
+    for store in stores:
+        store.wait()
 
 
 def call(kernel, outs, ins, scratch=(), cost=None, to="vmem", room=48):
@@ -626,14 +640,14 @@
     left = shifted(to_right, "rad", 1)
     right = shifted(to_left, "rad", -1)
     pick = jnp.asarray(pick_columns(radial))
-    return pl.pallas_call(
+    (result,) = call(
         final_kernel,
-        grid=(components,),
-        out_shape=jax.ShapeDtypeStruct(whole, jnp.float32),
-        in_specs=[pl.BlockSpec(memory_space=pltpu.VMEM)] * 7,
-        out_specs=pl.BlockSpec((1, azim, radial), lambda v: (v, 0, 0)),
-        compiler_params=pltpu.CompilerParams(vmem_limit_bytes=48 << 20),
+        [whole],
+        ["vmem"] * 7,
+        [pltpu.VMEM(whole, jnp.float32), pltpu.SemaphoreType.DMA((components,))],
+        to="hbm",
     )(inner, kappa, prior, nxt, left, right, pick)
+    return result
 
 
 def solution(mesh):

time: 68.5 us -> 64.9 us (0.947)
  Pallas kernels: 38.1 us -> 35.4 us
    pallas_call x1, Pallas kernels: 3.11 us -> 1.64 us  [local(): call(final_kernel, [whole], ['vmem'] * 7, [pltpu.VMEM(whole, jnp.float32)...]
    pallas_call x1, Pallas kernels: 18.3 us -> 16.9 us  [local(): call(functools.partial(rest_kernel, slots), [sums, face, strip, strip, (c...]
  transfers between devices with their start and end apart: 5 -> 5, of which waited for: 2 -> 2; matrix products, arithmetic and copies ran while one was open for 0% -> 0% of each run, Pallas kernels for 14% -> 16%
where the time goes in v1:
time: 64.9 us; the launch traced here: 64.6 us
  Pallas kernels  35.4 us (55%)
  starting transfers between devices  15.8 us (24%)
  waiting for transfers between devices  11 us (17%)
  local copies, waits for them, and re-layouts  2.27 us (3%)
    pallas_call x1, Pallas kernels, local(): call(functools.partial(rest_kernel, slots), [sums, face, strip, strip, (c...  16.9 us
    ppermute x4, starting transfers between devices, shifted(): return lax.ppermute(strip, axis, pairs)  10.6 us
    pallas_call x1, Pallas kernels, local(): call(functools.partial(pack_kernel, slots, azim), [(seg_count, slots.rows...  6.64 us
    all_to_all x1, waiting for transfers between devices, local(): lax.all_to_all(sends, 'segaz', split_axis=0, concat_axis=0, tiled=True)  6.24 us
    pallas_call x1, Pallas kernels, local(): call(functools.partial(own_kernel, slots), [sums], ['hbm'], [pltpu.VMEM((...  5.52 us
    all_to_all x1, starting transfers between devices, local(): lax.all_to_all(sends, 'segaz', split_axis=0, concat_axis=0, tiled=True)  5.14 us
    ppermute x4, waiting for transfers between devices, shifted(): return lax.ppermute(strip, axis, pairs)  4.73 us
    pallas_call x1, Pallas kernels, local(): call(inner_kernel, [whole], ['vmem'] * 4, cost=1 << 22)  3.43 us
  transfers between devices with their start and end apart: 5, of which 2 were waited for; matrix products, arithmetic and copies ran while one was open for 0% of the time, Pallas kernels for 16%

profile of v1, /device:TPU:19, one launch (start us, length us, event | category | flops | bytes accessed | tf_op | source)
XLA Modules:
  0.0 64.6 jit_solution(10245342300387144557)
XLA Ops:
  0.0 6.6 %shard_map.109.sends_hbm = f32[8,288,128]{2,1,0:T(8,128)} custom-call(s32[1,8]{1,0:T(1,128)} %count_hbm.1, f32[5,32768]{1,0:T(8,128)} %src_hbm.1, s32[256,128]{1,0:T(8,128)} %bitcast.1, f32[5,256,256]{2,1,0:T(8,128)} %face_ref.1), custom_call_target="tpu_custom_call" | custom-call | tf_op jit(solution)/shard_map/pallas_call | solution.py:590
  6.6 0.0 copy-start
  6.7 0.0 copy-start.5
  6.7 5.1 %all-to-all-start = ((f32[8,288,128]{2,1,0:T(8,128)}), f32[8,288,128]{2,1,0:T(8,128)}, u32[]{:S(2)}, u32[]{:S(2)}) async-start(f32[8,288,128]{2,1,0:T(8,128)} %shard_map.109.sends_hbm), calls=%async_computation | async-start | bytes 2359296 | tf_op jit(solution)/shard_map/all_to_all | solution.py:607
  11.8 0.0 copy-done
  11.8 0.0 copy-done.5
  11.8 0.0 copy-start.1
  11.8 1.3 %shard_map.111 = (f32[5,256,256]{2,1,0:T(8,128)S(1)}, f32[5,8,256]{2,1,0:T(8,128)S(1)}) custom-call(f32[5,256,256]{2,1,0:T(8,128)S(1)} %copy-done, f32[256,256]{1,0:T(8,128)S(1)} %copy-done.5), custom_call_target="tpu_custom_call" | custom-call | flops 4194304 | bytes 4194 | tf_op jit(solution)/shard_map/pallas_call | solution.py:626
  13.1 0.0 copy-start.3
  13.1 1.0 %copy-done.3 = f32[5,256,256]{2,1,0:T(8,128)} copy-done((f32[5,256,256]{2,1,0:T(8,128)}, f32[5,256,256]{2,1,0:T(8,128)S(1)}, u32[]{:S(2)}) %copy-start.3) | copy-done | bytes 1310744
  14.2 0.0 copy-done.1
  14.2 0.0 copy-start.6
  14.2 0.0 copy-start.9
  14.2 0.0 copy-start.10
  14.2 0.0 copy-start.11
  14.2 5.5 %shard_map.110.begun_ref = f32[5,304,256]{2,1,0:T(8,128)S(1)} custom-call(f32[8,288,128]{2,1,0:T(8,128)S(1)} %copy-done.1), custom_call_target="tpu_custom_call" | custom-call | flops 8388608 | bytes 8388 | tf_op jit(solution)/shard_map/pallas_call | solution.py:619
  19.7 0.0 copy-start.2
  19.8 1.2 %copy-done.2 = f32[5,304,256]{2,1,0:T(8,128)} copy-done((f32[5,304,256]{2,1,0:T(8,128)}, f32[5,304,256]{2,1,0:T(8,128)S(1)}, u32[]{:S(2)}) %copy-start.2) | copy-done | bytes 1556504
  20.9 6.2 %all-to-all-done.got_ref = f32[8,288,128]{2,1,0:T(8,128)} async-done(((f32[8,288,128]{2,1,0:T(8,128)}), f32[8,288,128]{2,1,0:T(8,128)}, u32[]{:S(2)}, u32[]{:S(2)}) %all-to-all-start) | async-done | bytes 1179680 | tf_op jit(solution)/shard_map/all_to_all | solution.py:607
  27.2 0.0 copy-done.6
  27.2 0.0 copy-done.9
  27.2 0.0 copy-done.10
  27.2 0.0 copy-done.11
  27.2 0.0 copy-start.4
  27.2 0.0 copy-start.7
  27.2 16.9 %shard_map.112 = (f32[5,304,256]{2,1,0:T(8,128)S(1)}, f32[5,8,256]{2,1,0:T(8,128)S(1)}, f32[5,8,512]{2,1,0:T(8,128)S(1)}, f32[5,8,512]{2,1,0:T(8,128)S(1)}, f32[5,16,256]{2,1,0:T(8,128)S(1)}) custom-call(s32[8]{0:T(128)S(1)} %copy-done.10, s32[8]{0:T(128)S(1)} %copy-done.11, f32[8,288,128]{2,1,0:T(8,128)} %all-to-all-done.got_ref, f32[5,304,256]{2,1,0:T(8,128)} %copy-done.2, ...), custom_call_target="tpu_custom_call" | custom-call | tf_op jit(solution)/shard_map/pallas_call | solution.py:630
  44.1 3.4 %collective-permute-start = (f32[5,8,512]{2,1,0:T(8,128)S(1)}, f32[5,8,512]{2,1,0:T(8,128)S(1)}, u32[]{:S(2)}, u32[]{:S(2)}) collective-permute-start(f32[5,8,512]{2,1,0:T(8,128)S(1)} %get-tuple-element.18), channel_id=1, source_target_pairs={{0,4},{4,8},{8,12},{12,16},{16,20},{20,24},{24,28},{1,5},{5,9},{9,... | collective-permute-start | bytes 245768 | tf_op jit(solution)/shard_map/ppermute | solution.py:575
  47.5 1.9 %collective-permute-start.1 = (f32[5,8,512]{2,1,0:T(8,128)S(1)}, f32[5,8,512]{2,1,0:T(8,128)S(1)}, u32[]{:S(2)}, u32[]{:S(2)}) collective-permute-start(f32[5,8,512]{2,1,0:T(8,128)S(1)} %get-tuple-element.19), channel_id=1, source_target_pairs={{4,0},{8,4},{12,8},{16,12},{20,16},{24,20},{28,24},{5,1},{9,5},{13... | collective-permute-start | bytes 245768 | tf_op jit(solution)/shard_map/ppermute | solution.py:575
  49.4 0.0 collective-permute-done.prior_ref
  49.4 4.7 %collective-permute-done.1.next_ref = f32[5,8,512]{2,1,0:T(8,128)S(1)} collective-permute-done((f32[5,8,512]{2,1,0:T(8,128)S(1)}, f32[5,8,512]{2,1,0:T(8,128)S(1)}, u32[]{:S(2)}, u32[]{:S(2)}) %collective-permute-start.1) | collective-permute-done | bytes 81952 | tf_op jit(solution)/shard_map/ppermute | solution.py:575
  54.2 3.2 %collective-permute-start.2 = (f32[5,8,256]{2,1,0:T(8,128)S(1)}, f32[5,8,256]{2,1,0:T(8,128)S(1)}, u32[]{:S(2)}, u32[]{:S(2)}) collective-permute-start(f32[5,8,256]{2,1,0:T(8,128)S(1)} %get-tuple-element.21), channel_id=1, source_target_pairs={{0,1},{1,2},{2,3},{4,5},{5,6},{6,7},{8,9},{9,10},{10,11},{12,13},{... | collective-permute-start | bytes 122888 | tf_op jit(solution)/shard_map/ppermute | solution.py:575
  57.4 2.1 %collective-permute-start.3 = (f32[5,8,256]{2,1,0:T(8,128)S(1)}, f32[5,8,256]{2,1,0:T(8,128)S(1)}, u32[]{:S(2)}, u32[]{:S(2)}) collective-permute-start(f32[5,8,256]{2,1,0:T(8,128)S(1)} %get-tuple-element.22), channel_id=1, source_target_pairs={{1,0},{2,1},{3,2},{5,4},{6,5},{7,6},{9,8},{10,9},{11,10},{13,12},{... | collective-permute-start | bytes 122888 | tf_op jit(solution)/shard_map/ppermute | solution.py:575
  59.5 0.0 copy-done.4
  59.5 0.0 copy-done.7
  59.5 0.0 copy-start.8
  59.5 3.4 %shard_map.113.inner_ref = f32[5,256,256]{2,1,0:T(8,128)S(1)} custom-call(f32[5,304,256]{2,1,0:T(8,128)S(1)} %get-tuple-element.15.sum_ref, f32[5,256,256]{2,1,0:T(8,128)S(1)} %copy-done.4, f32[5,8,256]{2,1,0:T(8,128)S(1)} %get-tuple-element.17.joint_ref, f32[256,256]{1,0:T(8,128)S(1)} %copy-done.7), custom_call_target="tpu_custom_call" | custom-call | flops 4194304 | bytes 4194 | tf_op jit(solution)/shard_map/pallas_call | solution.py:638
  63.0 0.0 collective-permute-done.2.left_ref
  63.0 0.0 collective-permute-done.3.right_ref
  63.0 0.0 copy-done.8
  63.0 1.6 %shard_map.115 = f32[5,256,256]{2,1,0:T(8,128)} custom-call(f32[5,256,256]{2,1,0:T(8,128)S(1)} %shard_map.113.inner_ref, f32[256,256]{1,0:T(8,128)S(1)} %copy-done.5, f32[5,8,512]{2,1,0:T(8,128)S(1)} %collective-permute-done.prior_ref, f32[5,8,512]{2,1,0:T(8,128)S(1)} %collective-permute-done.1.next_ref, f32[5,8,256]{2,1,0:T(8,128)S(1)} %collective-permute-done.2.left_ref, ...), custom_call_target="tpu_custom_call" | custom-call | tf_op jit(solution)/shard_map/pallas_call | solution.py:643
  (1 shorter events, 0.0 us)
Async XLA Ops:
  6.6 5.2 %copy-start = (f32[5,256,256]{2,1,0:T(8,128)S(1)}, f32[5,256,256]{2,1,0:T(8,128)}, u32[]{:S(2)}) copy-start(f32[5,256,256]{2,1,0:T(8,128)} %face_ref.1) | copy-start | bytes 3932164
  6.7 5.2 %copy-start.5 = (f32[256,256]{1,0:T(8,128)S(1)}, f32[256,256]{1,0:T(8,128)}, u32[]{:S(2)}) copy-start(f32[256,256]{1,0:T(8,128)} %kappa_ref.3) | copy-start | bytes 786436
  6.7 20.5 %all-to-all-start = ((f32[8,288,128]{2,1,0:T(8,128)}), f32[8,288,128]{2,1,0:T(8,128)}, u32[]{:S(2)}, u32[]{:S(2)}) async-start(f32[8,288,128]{2,1,0:T(8,128)} %shard_map.109.sends_hbm), calls=%async_computation | async-start | bytes 2359296 | tf_op jit(solution)/shard_map/all_to_all | solution.py:607
  11.8 2.4 %copy-start.1 = (f32[8,288,128]{2,1,0:T(8,128)S(1)}, f32[8,288,128]{2,1,0:T(8,128)}, u32[]{:S(2)}) copy-start(f32[8,288,128]{2,1,0:T(8,128)} %shard_map.109.sends_hbm) | copy-start | bytes 3538948
  13.1 1.1 %copy-start.3 = (f32[5,256,256]{2,1,0:T(8,128)}, f32[5,256,256]{2,1,0:T(8,128)S(1)}, u32[]{:S(2)}) copy-start(f32[5,256,256]{2,1,0:T(8,128)S(1)} %get-tuple-element.16.base_ref) | copy-start | bytes 3932164
  14.2 13.0 %copy-start.6 = (f32[256,512]{1,0:T(8,128)S(1)}, f32[256,512]{1,0:T(8,128)}, u32[]{:S(2)}) copy-start(f32[256,512]{1,0:T(8,128)} %constant.9.clone.far_ref) | copy-start | bytes 1572868
  14.2 13.0 %copy-start.9 = (f32[16,256]{1,0:T(8,128)S(1)}, f32[16,256]{1,0:T(8,128)}, u32[]{:S(2)}) copy-start(f32[16,256]{1,0:T(8,128)} %constant.8.clone.near_ref) | copy-start | bytes 49156
  14.2 13.0 %copy-start.10 = (s32[8]{0:T(128)S(1)}, s32[8]{0:T(128)}, u32[]{:S(2)}) copy-start(s32[8]{0:T(128)} %map_ref.1) | copy-start | bytes 100
  14.2 13.0 %copy-start.11 = (s32[8]{0:T(128)S(1)}, s32[8]{0:T(128)}, u32[]{:S(2)}) copy-start(s32[8]{0:T(128)} %match_ref.1) | copy-start | bytes 100
  19.7 1.2 %copy-start.2 = (f32[5,304,256]{2,1,0:T(8,128)}, f32[5,304,256]{2,1,0:T(8,128)S(1)}, u32[]{:S(2)}) copy-start(f32[5,304,256]{2,1,0:T(8,128)S(1)} %shard_map.110.begun_ref) | copy-start | bytes 4669444
  27.2 32.3 %copy-start.4 = (f32[5,256,256]{2,1,0:T(8,128)S(1)}, f32[5,256,256]{2,1,0:T(8,128)}, u32[]{:S(2)}) copy-start(f32[5,256,256]{2,1,0:T(8,128)} %copy-done.3) | copy-start | bytes 3932164
  27.2 32.3 %copy-start.7 = (f32[256,256]{1,0:T(8,128)S(1)}, f32[256,256]{1,0:T(8,128)}, u32[]{:S(2)}) copy-start(f32[256,256]{1,0:T(8,128)} %constant.10.clone.band_ref) | copy-start | bytes 786436
  44.1 5.4 %collective-permute-start = (f32[5,8,512]{2,1,0:T(8,128)S(1)}, f32[5,8,512]{2,1,0:T(8,128)S(1)}, u32[]{:S(2)}, u32[]{:S(2)}) collective-permute-start(f32[5,8,512]{2,1,0:T(8,128)S(1)} %get-tuple-element.18), channel_id=1, source_target_pairs={{0,4},{4,8},{8,12},{12,16},{16,20},{20,24},{24,28},{1,5},{5,9},{9,... | collective-permute-start | bytes 245768 | tf_op jit(solution)/shard_map/ppermute | solution.py:575
  47.5 6.7 %collective-permute-start.1 = (f32[5,8,512]{2,1,0:T(8,128)S(1)}, f32[5,8,512]{2,1,0:T(8,128)S(1)}, u32[]{:S(2)}, u32[]{:S(2)}) collective-permute-start(f32[5,8,512]{2,1,0:T(8,128)S(1)} %get-tuple-element.19), channel_id=1, source_target_pairs={{4,0},{8,4},{12,8},{16,12},{20,16},{24,20},{28,24},{5,1},{9,5},{13... | collective-permute-start | bytes 245768 | tf_op jit(solution)/shard_map/ppermute | solution.py:575
  54.2 8.8 %collective-permute-start.2 = (f32[5,8,256]{2,1,0:T(8,128)S(1)}, f32[5,8,256]{2,1,0:T(8,128)S(1)}, u32[]{:S(2)}, u32[]{:S(2)}) collective-permute-start(f32[5,8,256]{2,1,0:T(8,128)S(1)} %get-tuple-element.21), channel_id=1, source_target_pairs={{0,1},{1,2},{2,3},{4,5},{5,6},{6,7},{8,9},{9,10},{10,11},{12,13},{... | collective-permute-start | bytes 122888 | tf_op jit(solution)/shard_map/ppermute | solution.py:575
  57.4 5.6 %collective-permute-start.3 = (f32[5,8,256]{2,1,0:T(8,128)S(1)}, f32[5,8,256]{2,1,0:T(8,128)S(1)}, u32[]{:S(2)}, u32[]{:S(2)}) collective-permute-start(f32[5,8,256]{2,1,0:T(8,128)S(1)} %get-tuple-element.22), channel_id=1, source_target_pairs={{1,0},{2,1},{3,2},{5,4},{6,5},{7,6},{9,8},{10,9},{11,10},{13,12},{... | collective-permute-start | bytes 122888 | tf_op jit(solution)/shard_map/ppermute | solution.py:575
  59.5 3.5 %copy-start.8 = (f32[16,512]{1,0:T(8,128)S(1)}, f32[16,512]{1,0:T(8,128)}, u32[]{:S(2)}) copy-start(f32[16,512]{1,0:T(8,128)} %constant.11.clone.pick_ref) | copy-start | bytes 98308

commit v2 on v1

--- a/solution.py
+++ b/solution.py
@@ -15,6 +15,8 @@
 ROUNDS = 6
 UNROLL = 16
 OWN_UNROLL = 5
+SPARE = 8
+FEW = 4
 STEP = 4
 PIECES = 4
 HALF = 64
@@ -337,7 +339,7 @@
     return -(-(chunks * (256 // WINDOW + 1) + UNROLL) // LANES) * LANES
 
 
-def add_chunks(slots, own, own_only, got_ref, sum_ref, list_ref, task_ref, order_ref, work_ref, sems):
+def add_chunks(slots, own, own_only, meanwhile, got_ref, sum_ref, list_ref, task_ref, order_ref, work_ref, sems):
     seg_count = got_ref.shape[0]
     components, _, radial = sum_ref.shape
     azim = sum_ref.shape[1] - WINDOW
@@ -366,6 +368,7 @@
     ]
     for copy in copies:
         copy.start()
+    meanwhile()
     cells = lax.broadcasted_iota(jnp.int32, (radial, width), 0).astype(jnp.float32).astype(jnp.bfloat16)
     near = lax.broadcasted_iota(jnp.int32, (WINDOW, width), 0).astype(jnp.float32).astype(jnp.bfloat16)
     lanes = lax.broadcasted_iota(jnp.int32, (1, width), 1)
@@ -401,23 +404,33 @@
         part = part[: components * WINDOW] + part[components * WINDOW :]
         return start, part
 
-    def several(t, carry):
-        done = [block(t * unroll + u) for u in range(unroll)]
+    def several(first, size):
+        done = [block(first + u) for u in range(size)]
         for start, part in done:
             for v in range(components):
                 sum_ref[v, pl.ds(start, WINDOW), :] += part[v * WINDOW : (v + 1) * WINDOW]
-        return carry
-
-    lax.fori_loop(0, (total + unroll - 1) // unroll, several, 0)
+
+    full = (total + unroll - 1 - (0 if own_only else SPARE)) // unroll
+
+    @pl.loop(0, full)
+    def _(t):
+        several(t * unroll, unroll)
+
+    @pl.loop(0, (jnp.maximum(total - full * unroll, 0) + FEW - 1) // FEW)
+    def _(t):
+        several(full * unroll + t * FEW, FEW)
 
 
 def own_kernel(slots, sends_hbm, sum_ref, held_ref, *work):
     own = lax.axis_index("segaz")
     load = pltpu.make_async_copy(sends_hbm.at[own], held_ref.at[0], work[-1])
     load.start()
-    sum_ref[...] = jnp.zeros(sum_ref.shape, jnp.float32)
+
+    def meanwhile():
+        sum_ref[...] = jnp.zeros(sum_ref.shape, jnp.float32)
+
     load.wait()
-    add_chunks(slots, own, True, held_ref, sum_ref, *work[:-1])
+    add_chunks(slots, own, True, meanwhile, held_ref, sum_ref, *work[:-1])
 
 
 def rest_kernel(
@@ -429,23 +442,25 @@
     seg_count = got_ref.shape[0]
     components, _, radial = sum_ref.shape
     azim = sum_ref.shape[1] - WINDOW
-    sum_ref[...] = begun_ref[...]
     own = lax.axis_index("segaz")
-    add_chunks(slots, own, False, got_ref, sum_ref, *work)
-
-    partner = jnp.int32(0)
-    target = match_ref[map_ref[own]]
-    for h in range(seg_count):
-        partner = jnp.where(map_ref[h] == target, h, partner)
-    layer = lax.broadcasted_iota(jnp.int32, (JL, radial), 0)
-    strength = jnp.zeros((JL, radial), jnp.float32)
-    for l in range(JL):
-        strength = jnp.where(layer == l, layer_weights[l], strength)
-    for v in range(components):
-        tile = got_ref[partner, slots.face + 8 * v : slots.face + 8 * v + 8, :]
-        face = jnp.concatenate([tile[:JL], tile[JL:]], axis=1)
-        joint_ref[v, 0:JL, :] = strength * (face - face_ref[v, 0:JL, :])
-        joint_ref[v, JL:8, :] = jnp.zeros((8 - JL, radial), jnp.float32)
+
+    def meanwhile():
+        sum_ref[...] = begun_ref[...]
+        partner = jnp.int32(0)
+        target = match_ref[map_ref[own]]
+        for h in range(seg_count):
+            partner = jnp.where(map_ref[h] == target, h, partner)
+        layer = lax.broadcasted_iota(jnp.int32, (JL, radial), 0)
+        strength = jnp.zeros((JL, radial), jnp.float32)
+        for l in range(JL):
+            strength = jnp.where(layer == l, layer_weights[l], strength)
+        for v in range(components):
+            tile = got_ref[partner, slots.face + 8 * v : slots.face + 8 * v + 8, :]
+            face = jnp.concatenate([tile[:JL], tile[JL:]], axis=1)
+            joint_ref[v, 0:JL, :] = strength * (face - face_ref[v, 0:JL, :])
+            joint_ref[v, JL:8, :] = jnp.zeros((8 - JL, radial), jnp.float32)
+
+    add_chunks(slots, own, False, meanwhile, got_ref, sum_ref, *work)
 
     near = halves(near_ref[...])
     far = halves(far_ref[...])

time: 64.9 us -> 64.9 us (level)
  Pallas kernels: 35.4 us -> 33.6 us
  waiting for transfers between devices: 11 us -> 11.9 us
  starting transfers between devices: 15.8 us -> 16.6 us
    all_to_all x1, waiting for transfers between devices: 6.24 us -> 7.21 us  [local(): lax.all_to_all(sends, 'segaz', split_axis=0, concat_axis=0, tiled=True)]
    pallas_call x1, Pallas kernels: 5.52 us -> 4.55 us  [local(): call(functools.partial(own_kernel, slots), [sums], ['hbm'], [pltpu.VMEM((...]
    ppermute x4, starting transfers between devices: 10.6 us -> 11.5 us  [shifted(): return lax.ppermute(strip, axis, pairs)]
    pallas_call x1, Pallas kernels: 16.9 us -> 16 us  [local(): call(functools.partial(rest_kernel, slots), [sums, face, strip, strip, (c...]
  transfers between devices with their start and end apart: 5 -> 5, of which waited for: 2 -> 2; matrix products, arithmetic and copies ran while one was open for 0% -> 0% of each run, Pallas kernels for 16% -> 14%
where the time goes in v2:
time: 64.9 us; the launch traced here: 64.6 us
  Pallas kernels  33.6 us (52%)
  starting transfers between devices  16.6 us (26%)
  waiting for transfers between devices  11.9 us (18%)
  local copies, waits for them, and re-layouts  2.27 us (3%)
    pallas_call x1, Pallas kernels, local(): call(functools.partial(rest_kernel, slots), [sums, face, strip, strip, (c...  16 us
    ppermute x4, starting transfers between devices, shifted(): return lax.ppermute(strip, axis, pairs)  11.5 us
    all_to_all x1, waiting for transfers between devices, local(): lax.all_to_all(sends, 'segaz', split_axis=0, concat_axis=0, tiled=True)  7.21 us
    pallas_call x1, Pallas kernels, local(): call(functools.partial(pack_kernel, slots, azim), [(seg_count, slots.rows...  6.64 us
    all_to_all x1, starting transfers between devices, local(): lax.all_to_all(sends, 'segaz', split_axis=0, concat_axis=0, tiled=True)  5.14 us
    ppermute x4, waiting for transfers between devices, shifted(): return lax.ppermute(strip, axis, pairs)  4.73 us
    pallas_call x1, Pallas kernels, local(): call(functools.partial(own_kernel, slots), [sums], ['hbm'], [pltpu.VMEM((...  4.55 us
    pallas_call x1, Pallas kernels, local(): call(inner_kernel, [whole], ['vmem'] * 4, cost=1 << 22)  3.43 us
  transfers between devices with their start and end apart: 5, of which 2 were waited for; matrix products, arithmetic and copies ran while one was open for 0% of the time, Pallas kernels for 14%

profile of v2, /device:TPU:19, one launch (start us, length us, event | category | flops | bytes accessed | tf_op | source)
XLA Modules:
  0.0 64.6 jit_solution(17355016416114153148)
XLA Ops:
  0.0 6.6 %shard_map.109.sends_hbm = f32[8,288,128]{2,1,0:T(8,128)} custom-call(s32[1,8]{1,0:T(1,128)} %count_hbm.1, f32[5,32768]{1,0:T(8,128)} %src_hbm.1, s32[256,128]{1,0:T(8,128)} %bitcast.1, f32[5,256,256]{2,1,0:T(8,128)} %face_ref.1), custom_call_target="tpu_custom_call" | custom-call | tf_op jit(solution)/shard_map/pallas_call | solution.py:605
  6.6 0.0 copy-start
  6.7 0.0 copy-start.5
  6.7 5.1 %all-to-all-start = ((f32[8,288,128]{2,1,0:T(8,128)}), f32[8,288,128]{2,1,0:T(8,128)}, u32[]{:S(2)}, u32[]{:S(2)}) async-start(f32[8,288,128]{2,1,0:T(8,128)} %shard_map.109.sends_hbm), calls=%async_computation | async-start | bytes 2359296 | tf_op jit(solution)/shard_map/all_to_all | solution.py:622
  11.8 0.0 copy-done
  11.8 0.0 copy-done.5
  11.8 0.0 copy-start.1
  11.8 1.3 %shard_map.111 = (f32[5,256,256]{2,1,0:T(8,128)S(1)}, f32[5,8,256]{2,1,0:T(8,128)S(1)}) custom-call(f32[5,256,256]{2,1,0:T(8,128)S(1)} %copy-done, f32[256,256]{1,0:T(8,128)S(1)} %copy-done.5), custom_call_target="tpu_custom_call" | custom-call | flops 4194304 | bytes 4194 | tf_op jit(solution)/shard_map/pallas_call | solution.py:641
  13.1 0.0 copy-start.3
  13.1 1.0 %copy-done.3 = f32[5,256,256]{2,1,0:T(8,128)} copy-done((f32[5,256,256]{2,1,0:T(8,128)}, f32[5,256,256]{2,1,0:T(8,128)S(1)}, u32[]{:S(2)}) %copy-start.3) | copy-done | bytes 1310744
  14.2 0.0 copy-done.1
  14.2 0.0 copy-start.6
  14.2 0.0 copy-start.9
  14.2 0.0 copy-start.10
  14.2 0.0 copy-start.11
  14.2 4.5 %shard_map.110.begun_ref = f32[5,304,256]{2,1,0:T(8,128)S(1)} custom-call(f32[8,288,128]{2,1,0:T(8,128)S(1)} %copy-done.1), custom_call_target="tpu_custom_call" | custom-call | flops 8388608 | bytes 8388 | tf_op jit(solution)/shard_map/pallas_call | solution.py:634
  18.8 0.0 copy-start.2
  18.8 1.2 %copy-done.2 = f32[5,304,256]{2,1,0:T(8,128)} copy-done((f32[5,304,256]{2,1,0:T(8,128)}, f32[5,304,256]{2,1,0:T(8,128)S(1)}, u32[]{:S(2)}) %copy-start.2) | copy-done | bytes 1556504
  19.9 7.2 %all-to-all-done.got_ref = f32[8,288,128]{2,1,0:T(8,128)} async-done(((f32[8,288,128]{2,1,0:T(8,128)}), f32[8,288,128]{2,1,0:T(8,128)}, u32[]{:S(2)}, u32[]{:S(2)}) %all-to-all-start) | async-done | bytes 1179680 | tf_op jit(solution)/shard_map/all_to_all | solution.py:622
  27.2 0.0 copy-done.6
  27.2 0.0 copy-done.9
  27.2 0.0 copy-done.10
  27.2 0.0 copy-done.11
  27.2 0.0 copy-start.4
  27.2 0.0 copy-start.7
  27.2 16.0 %shard_map.112 = (f32[5,304,256]{2,1,0:T(8,128)S(1)}, f32[5,8,256]{2,1,0:T(8,128)S(1)}, f32[5,8,512]{2,1,0:T(8,128)S(1)}, f32[5,8,512]{2,1,0:T(8,128)S(1)}, f32[5,16,256]{2,1,0:T(8,128)S(1)}) custom-call(s32[8]{0:T(128)S(1)} %copy-done.10, s32[8]{0:T(128)S(1)} %copy-done.11, f32[8,288,128]{2,1,0:T(8,128)} %all-to-all-done.got_ref, f32[5,304,256]{2,1,0:T(8,128)} %copy-done.2, ...), custom_call_target="tpu_custom_call" | custom-call | tf_op jit(solution)/shard_map/pallas_call | solution.py:645
  43.2 4.3 %collective-permute-start = (f32[5,8,512]{2,1,0:T(8,128)S(1)}, f32[5,8,512]{2,1,0:T(8,128)S(1)}, u32[]{:S(2)}, u32[]{:S(2)}) collective-permute-start(f32[5,8,512]{2,1,0:T(8,128)S(1)} %get-tuple-element.18), channel_id=1, source_target_pairs={{0,4},{4,8},{8,12},{12,16},{16,20},{20,24},{24,28},{1,5},{5,9},{9,... | collective-permute-start | bytes 245768 | tf_op jit(solution)/shard_map/ppermute | solution.py:590
  47.5 1.9 %collective-permute-start.1 = (f32[5,8,512]{2,1,0:T(8,128)S(1)}, f32[5,8,512]{2,1,0:T(8,128)S(1)}, u32[]{:S(2)}, u32[]{:S(2)}) collective-permute-start(f32[5,8,512]{2,1,0:T(8,128)S(1)} %get-tuple-element.19), channel_id=1, source_target_pairs={{4,0},{8,4},{12,8},{16,12},{20,16},{24,20},{28,24},{5,1},{9,5},{13... | collective-permute-start | bytes 245768 | tf_op jit(solution)/shard_map/ppermute | solution.py:590
  49.4 0.0 collective-permute-done.prior_ref
  49.4 4.7 %collective-permute-done.1.next_ref = f32[5,8,512]{2,1,0:T(8,128)S(1)} collective-permute-done((f32[5,8,512]{2,1,0:T(8,128)S(1)}, f32[5,8,512]{2,1,0:T(8,128)S(1)}, u32[]{:S(2)}, u32[]{:S(2)}) %collective-permute-start.1) | collective-permute-done | bytes 81952 | tf_op jit(solution)/shard_map/ppermute | solution.py:590
  54.2 1.9 %collective-permute-start.2 = (f32[5,8,256]{2,1,0:T(8,128)S(1)}, f32[5,8,256]{2,1,0:T(8,128)S(1)}, u32[]{:S(2)}, u32[]{:S(2)}) collective-permute-start(f32[5,8,256]{2,1,0:T(8,128)S(1)} %get-tuple-element.21), channel_id=1, source_target_pairs={{0,1},{1,2},{2,3},{4,5},{5,6},{6,7},{8,9},{9,10},{10,11},{12,13},{... | collective-permute-start | bytes 122888 | tf_op jit(solution)/shard_map/ppermute | solution.py:590
  56.1 3.4 %collective-permute-start.3 = (f32[5,8,256]{2,1,0:T(8,128)S(1)}, f32[5,8,256]{2,1,0:T(8,128)S(1)}, u32[]{:S(2)}, u32[]{:S(2)}) collective-permute-start(f32[5,8,256]{2,1,0:T(8,128)S(1)} %get-tuple-element.22), channel_id=1, source_target_pairs={{1,0},{2,1},{3,2},{5,4},{6,5},{7,6},{9,8},{10,9},{11,10},{13,12},{... | collective-permute-start | bytes 122888 | tf_op jit(solution)/shard_map/ppermute | solution.py:590
  59.5 0.0 copy-done.4
  59.5 0.0 copy-done.7
  59.5 0.0 copy-start.8
  59.5 3.4 %shard_map.113.inner_ref = f32[5,256,256]{2,1,0:T(8,128)S(1)} custom-call(f32[5,304,256]{2,1,0:T(8,128)S(1)} %get-tuple-element.15.sum_ref, f32[5,256,256]{2,1,0:T(8,128)S(1)} %copy-done.4, f32[5,8,256]{2,1,0:T(8,128)S(1)} %get-tuple-element.17.joint_ref, f32[256,256]{1,0:T(8,128)S(1)} %copy-done.7), custom_call_target="tpu_custom_call" | custom-call | flops 4194304 | bytes 4194 | tf_op jit(solution)/shard_map/pallas_call | solution.py:653
  63.0 0.0 collective-permute-done.2.left_ref
  63.0 0.0 collective-permute-done.3.right_ref
  63.0 0.0 copy-done.8
  63.0 1.6 %shard_map.115 = f32[5,256,256]{2,1,0:T(8,128)} custom-call(f32[5,256,256]{2,1,0:T(8,128)S(1)} %shard_map.113.inner_ref, f32[256,256]{1,0:T(8,128)S(1)} %copy-done.5, f32[5,8,512]{2,1,0:T(8,128)S(1)} %collective-permute-done.prior_ref, f32[5,8,512]{2,1,0:T(8,128)S(1)} %collective-permute-done.1.next_ref, f32[5,8,256]{2,1,0:T(8,128)S(1)} %collective-permute-done.2.left_ref, ...), custom_call_target="tpu_custom_call" | custom-call | tf_op jit(solution)/shard_map/pallas_call | solution.py:658
  (1 shorter events, 0.0 us)
Async XLA Ops:
  6.6 5.2 %copy-start = (f32[5,256,256]{2,1,0:T(8,128)S(1)}, f32[5,256,256]{2,1,0:T(8,128)}, u32[]{:S(2)}) copy-start(f32[5,256,256]{2,1,0:T(8,128)} %face_ref.1) | copy-start | bytes 3932164
  6.7 5.2 %copy-start.5 = (f32[256,256]{1,0:T(8,128)S(1)}, f32[256,256]{1,0:T(8,128)}, u32[]{:S(2)}) copy-start(f32[256,256]{1,0:T(8,128)} %kappa_ref.3) | copy-start | bytes 786436
  6.7 20.5 %all-to-all-start = ((f32[8,288,128]{2,1,0:T(8,128)}), f32[8,288,128]{2,1,0:T(8,128)}, u32[]{:S(2)}, u32[]{:S(2)}) async-start(f32[8,288,128]{2,1,0:T(8,128)} %shard_map.109.sends_hbm), calls=%async_computation | async-start | bytes 2359296 | tf_op jit(solution)/shard_map/all_to_all | solution.py:622
  11.8 2.4 %copy-start.1 = (f32[8,288,128]{2,1,0:T(8,128)S(1)}, f32[8,288,128]{2,1,0:T(8,128)}, u32[]{:S(2)}) copy-start(f32[8,288,128]{2,1,0:T(8,128)} %shard_map.109.sends_hbm) | copy-start | bytes 3538948
  13.1 1.1 %copy-start.3 = (f32[5,256,256]{2,1,0:T(8,128)}, f32[5,256,256]{2,1,0:T(8,128)S(1)}, u32[]{:S(2)}) copy-start(f32[5,256,256]{2,1,0:T(8,128)S(1)} %get-tuple-element.16.base_ref) | copy-start | bytes 3932164
  14.2 13.0 %copy-start.6 = (f32[256,512]{1,0:T(8,128)S(1)}, f32[256,512]{1,0:T(8,128)}, u32[]{:S(2)}) copy-start(f32[256,512]{1,0:T(8,128)} %constant.9.clone.far_ref) | copy-start | bytes 1572868
  14.2 13.0 %copy-start.9 = (f32[16,256]{1,0:T(8,128)S(1)}, f32[16,256]{1,0:T(8,128)}, u32[]{:S(2)}) copy-start(f32[16,256]{1,0:T(8,128)} %constant.8.clone.near_ref) | copy-start | bytes 49156
  14.2 13.0 %copy-start.10 = (s32[8]{0:T(128)S(1)}, s32[8]{0:T(128)}, u32[]{:S(2)}) copy-start(s32[8]{0:T(128)} %map_ref.1) | copy-start | bytes 100
  14.2 13.0 %copy-start.11 = (s32[8]{0:T(128)S(1)}, s32[8]{0:T(128)}, u32[]{:S(2)}) copy-start(s32[8]{0:T(128)} %match_ref.1) | copy-start | bytes 100
  18.8 1.2 %copy-start.2 = (f32[5,304,256]{2,1,0:T(8,128)}, f32[5,304,256]{2,1,0:T(8,128)S(1)}, u32[]{:S(2)}) copy-start(f32[5,304,256]{2,1,0:T(8,128)S(1)} %shard_map.110.begun_ref) | copy-start | bytes 4669444
  27.2 32.3 %copy-start.4 = (f32[5,256,256]{2,1,0:T(8,128)S(1)}, f32[5,256,256]{2,1,0:T(8,128)}, u32[]{:S(2)}) copy-start(f32[5,256,256]{2,1,0:T(8,128)} %copy-done.3) | copy-start | bytes 3932164
  27.2 32.3 %copy-start.7 = (f32[256,256]{1,0:T(8,128)S(1)}, f32[256,256]{1,0:T(8,128)}, u32[]{:S(2)}) copy-start(f32[256,256]{1,0:T(8,128)} %constant.10.clone.band_ref) | copy-start | bytes 786436
  43.2 6.2 %collective-permute-start = (f32[5,8,512]{2,1,0:T(8,128)S(1)}, f32[5,8,512]{2,1,0:T(8,128)S(1)}, u32[]{:S(2)}, u32[]{:S(2)}) collective-permute-start(f32[5,8,512]{2,1,0:T(8,128)S(1)} %get-tuple-element.18), channel_id=1, source_target_pairs={{0,4},{4,8},{8,12},{12,16},{16,20},{20,24},{24,28},{1,5},{5,9},{9,... | collective-permute-start | bytes 245768 | tf_op jit(solution)/shard_map/ppermute | solution.py:590
  47.5 6.7 %collective-permute-start.1 = (f32[5,8,512]{2,1,0:T(8,128)S(1)}, f32[5,8,512]{2,1,0:T(8,128)S(1)}, u32[]{:S(2)}, u32[]{:S(2)}) collective-permute-start(f32[5,8,512]{2,1,0:T(8,128)S(1)} %get-tuple-element.19), channel_id=1, source_target_pairs={{4,0},{8,4},{12,8},{16,12},{20,16},{24,20},{28,24},{5,1},{9,5},{13... | collective-permute-start | bytes 245768 | tf_op jit(solution)/shard_map/ppermute | solution.py:590
  54.2 8.8 %collective-permute-start.2 = (f32[5,8,256]{2,1,0:T(8,128)S(1)}, f32[5,8,256]{2,1,0:T(8,128)S(1)}, u32[]{:S(2)}, u32[]{:S(2)}) collective-permute-start(f32[5,8,256]{2,1,0:T(8,128)S(1)} %get-tuple-element.21), channel_id=1, source_target_pairs={{0,1},{1,2},{2,3},{4,5},{5,6},{6,7},{8,9},{9,10},{10,11},{12,13},{... | collective-permute-start | bytes 122888 | tf_op jit(solution)/shard_map/ppermute | solution.py:590
  56.1 6.9 %collective-permute-start.3 = (f32[5,8,256]{2,1,0:T(8,128)S(1)}, f32[5,8,256]{2,1,0:T(8,128)S(1)}, u32[]{:S(2)}, u32[]{:S(2)}) collective-permute-start(f32[5,8,256]{2,1,0:T(8,128)S(1)} %get-tuple-element.22), channel_id=1, source_target_pairs={{1,0},{2,1},{3,2},{5,4},{6,5},{7,6},{9,8},{10,9},{11,10},{13,12},{... | collective-permute-start | bytes 122888 | tf_op jit(solution)/shard_map/ppermute | solution.py:590
  59.5 3.5 %copy-start.8 = (f32[16,512]{1,0:T(8,128)S(1)}, f32[16,512]{1,0:T(8,128)}, u32[]{:S(2)}) copy-start(f32[16,512]{1,0:T(8,128)} %constant.11.clone.pick_ref) | copy-start | bytes 98308
